TPU v7x, 32 devices: a whole 2x2x4 slice. The times are simulated.
32 devices in a mesh: rep: 4 (over y, x), wide: 8 (over z, core).
Axes of the slice: x: 2, y: 2, z: 4, core: 2. Of those that a mesh axis runs over, the one named last changes fastest.
Arguments:
- decoder_input: bfloat16 [32, 1024, 512], P(('rep', 'wide')), may hold values from -6 to 6
- target_embed: bfloat16 [32, 1024, 512], P(('rep', 'wide')), may hold values from -6 to 6
- encoder_states: bfloat16 [32, 1024, 512], P(('rep', 'wide')), may hold values from -6 to 6
- sentence_ids: int32 [32, 1024], P(('rep', 'wide')), may hold values from 0 to 15, never falling along the last dimension, each value on 1 to 128 neighbouring positions
- position_ranks: int32 [32, 1024], P(('rep', 'wide')), may hold values from 0 to 127
- hamming_counts: int32 [32, 16], P(('rep', 'wide')), may hold values from 0 to 256
- output_grad: bfloat16 [32, 1024, 512], P(('rep', 'wide')), may hold values from -6 to 6
- attn_in: float32 [6, 512, 512], P(None, 'wide'), may hold values from -0.25 to 0.25
- attn_out: float32 [2, 512, 512], P(None, 'wide'), may hold values from -0.75 to 0.75
- ffn_in: float32 [1, 512, 2048], P(None, 'wide'), may hold values from -0.25 to 0.25
- ffn_out: float32 [1, 2048, 512], P(None, 'wide'), may hold values from -0.125 to 0.125
- small_params: float32 [11, 512], P(None, 'wide'), may hold values from -1.2 to 1.3, as said below
- attn_in_mom: float32 [6, 512, 512], P(None, 'wide'), may hold values from -0.3 to 0.3
- attn_out_mom: float32 [2, 512, 512], P(None, 'wide'), may hold values from -0.3 to 0.3
- ffn_in_mom: float32 [1, 512, 2048], P(None, 'wide'), may hold values from -0.3 to 0.3
- ffn_out_mom: float32 [1, 2048, 512], P(None, 'wide'), may hold values from -0.3 to 0.3
- small_mom: float32 [11, 512], P(None, 'wide'), may hold values from -0.3 to 0.3
- attn_in_err: float32 [4, 6, 512, 512], P('rep', None, 'wide'), may hold values from -5 to 5
- attn_out_err: float32 [4, 2, 512, 512], P('rep', None, 'wide'), may hold values from -5 to 5
- ffn_in_err: float32 [4, 1, 512, 2048], P('rep', None, 'wide'), may hold values from -5 to 5
- ffn_out_err: float32 [4, 1, 2048, 512], P('rep', None, 'wide'), may hold values from -5 to 5
- attn_in_fac: float32 [6, 512, 8], replicated, may hold values from -6 to 6
- attn_out_fac: float32 [2, 512, 8], replicated, may hold values from -6 to 6
- ffn_in_fac: float32 [1, 2048, 8], replicated, may hold values from -6 to 6
- ffn_out_fac: float32 [1, 512, 8], replicated, may hold values from -6 to 6
- attn_in_avg: float32 [6, 512, 512], P(None, 'wide'), may hold values from -0.25 to 0.25
- attn_out_avg: float32 [2, 512, 512], P(None, 'wide'), may hold values from -0.75 to 0.75
- ffn_in_avg: float32 [1, 512, 2048], P(None, 'wide'), may hold values from -0.25 to 0.25
- ffn_out_avg: float32 [1, 2048, 512], P(None, 'wide'), may hold values from -0.125 to 0.125
- small_avg: float32 [11, 512], P(None, 'wide'), may hold values from -1.2 to 1.3, as said below
Outputs:
- layer_out: bfloat16 [32, 1024, 512], P(('rep', 'wide'))
- input_grad: float32 [32, 1024, 512], P(('rep', 'wide'))
- attn_in_new: float32 [6, 512, 512], P(None, 'wide')
- attn_out_new: float32 [2, 512, 512], P(None, 'wide')
- ffn_in_new: float32 [1, 512, 2048], P(None, 'wide')
- ffn_out_new: float32 [1, 2048, 512], P(None, 'wide')
- small_new: float32 [11, 512], P(None, 'wide')
- attn_in_mom_new: float32 [6, 512, 512], P(None, 'wide')
- attn_out_mom_new: float32 [2, 512, 512], P(None, 'wide')
- ffn_in_mom_new: float32 [1, 512, 2048], P(None, 'wide')
- ffn_out_mom_new: float32 [1, 2048, 512], P(None, 'wide')
- small_mom_new: float32 [11, 512], P(None, 'wide')
- attn_in_err_new: float32 [4, 6, 512, 512], P('rep', None, 'wide')
- attn_out_err_new: float32 [4, 2, 512, 512], P('rep', None, 'wide')
- ffn_in_err_new: float32 [4, 1, 512, 2048], P('rep', None, 'wide')
- ffn_out_err_new: float32 [4, 1, 2048, 512], P('rep', None, 'wide')
- attn_in_fac_new: float32 [6, 512, 8], replicated
- attn_out_fac_new: float32 [2, 512, 8], replicated
- ffn_in_fac_new: float32 [1, 2048, 8], replicated
- ffn_out_fac_new: float32 [1, 512, 8], replicated
- attn_in_avg_new: float32 [6, 512, 512], P(None, 'wide')
- attn_out_avg_new: float32 [2, 512, 512], P(None, 'wide')
- ffn_in_avg_new: float32 [1, 512, 2048], P(None, 'wide')
- ffn_out_avg_new: float32 [1, 2048, 512], P(None, 'wide')
- small_avg_new: float32 [11, 512], P(None, 'wide')
Inputs may be any that keep to these rules, and one draw needn't show every extreme that they name: `small_params`: rows 0, 2 and 4 are the gains, within 0.7 to 1.3; the other rows are shifts and biases. `small_avg`: rows 0, 2 and 4 are the gains' averages, within 0.7 to 1.3.
All inputs are finite; a program needn't handle non-finite values.
Results may differ from a plain program's by a relative error of at most 0.02.
The roundings to bfloat16 on the way count: a program that leaves them out, or rounds other values in their place, can miss the bound.
Values may be sent and summed in bfloat16 or wider, within the bound.
A program may use at most 320 MiB of HBM per device.

v0:
```python
import jax
import jax.numpy as jnp
from jax import lax
from jax.sharding import PartitionSpec as P

HEADS = 8
HEAD_DIM = 64


FULL_PRECISION = lax.Precision.HIGHEST
MOMENTUM = 0.9
LEARN_RATE = 0.1
VECTOR_RATE = 0.5
AVERAGE = 0.25


def matmul(left_arr, right_arr):
    return jnp.dot(left_arr, right_arr, preferred_element_type=jnp.float32)


def contract_rows(left_arr, right_arr):
    return lax.dot_general(
        left_arr, right_arr, (((0,), (0,)), ((), ())), preferred_element_type=jnp.float32
    )


def times_transpose(left_arr, right_arr):
    return lax.dot_general(
        left_arr, right_arr, (((1,), (1,)), ((), ())), preferred_element_type=jnp.float32
    )


def gelu_exact(value):
    return 0.5 * value * (1.0 + lax.erf(value * 0.7071067811865476))


def gelu_slope(value):
    return (
        0.5 * (1.0 + lax.erf(value * 0.7071067811865476))
        + value * jnp.exp(-0.5 * value * value) * 0.3989422804014327
    )


def layer_norm(resid, gain, shift):
    center = resid - jnp.mean(resid, axis=-1, keepdims=True)
    inv_std = lax.rsqrt(jnp.mean(center * center, axis=-1, keepdims=True) + 1e-05)
    normed = center * inv_std
    return (normed * gain + shift, normed, inv_std)


def layer_norm_back(upstream, gain, normed, inv_std):
    scaled = upstream * gain
    resid_grad = inv_std * (
        scaled
        - jnp.mean(scaled, axis=-1, keepdims=True)
        - normed * jnp.mean(scaled * normed, axis=-1, keepdims=True)
    )
    return (resid_grad, jnp.sum(upstream * normed, axis=0), jnp.sum(upstream, axis=0))


def attend_forward(query_in, source, w_query, w_key, w_value, same_sentence):
    length = query_in.shape[0]
    block_rows = min(512, length)
    score_scale = HEAD_DIM ** (-0.5)
    query_heads = matmul(query_in, w_query).astype(jnp.bfloat16).reshape(length, HEADS, HEAD_DIM)
    key_heads = matmul(source, w_key).astype(jnp.bfloat16).reshape(length, HEADS, HEAD_DIM)
    value_heads = matmul(source, w_value).astype(jnp.bfloat16).reshape(length, HEADS, HEAD_DIM)
    pieces, totals = ([], [])
    for first_row in range(0, length, block_rows):
        scores = (
            jnp.einsum(
                "qhd,khd->hqk",
                query_heads[first_row : first_row + block_rows],
                key_heads,
                preferred_element_type=jnp.float32,
            )
            * score_scale
        )
        scores = jnp.where(
            same_sentence[first_row : first_row + block_rows][None], scores, -1000000000.0
        )
        row_peak = jnp.max(scores, axis=-1, keepdims=True)
        exponent = jnp.exp(scores - row_peak)
        row_total = jnp.sum(exponent, axis=-1, keepdims=True)
        attn_probs = (exponent / row_total).astype(jnp.bfloat16)
        pieces.append(
            jnp.einsum("hqk,khd->qhd", attn_probs, value_heads, preferred_element_type=jnp.float32)
        )
        totals.append(row_peak + jnp.log(row_total))
    mixed_out = (
        jnp.concatenate(pieces, axis=0).reshape(length, HEADS * HEAD_DIM).astype(jnp.bfloat16)
    )
    return (query_heads, key_heads, value_heads, mixed_out, jnp.concatenate(totals, axis=1))


def attend_backward(mixed_grad, query_heads, key_heads, value_heads, log_totals, same_sentence):
    length = query_heads.shape[0]
    block_rows = min(512, length)
    score_scale = HEAD_DIM ** (-0.5)
    grad_heads = mixed_grad.reshape(length, HEADS, HEAD_DIM)
    query_parts = []
    key_grad = jnp.zeros(key_heads.shape, jnp.float32)
    value_grad = jnp.zeros(value_heads.shape, jnp.float32)
    for first_row in range(0, length, block_rows):
        rows_query = query_heads[first_row : first_row + block_rows]
        rows_grad = grad_heads[first_row : first_row + block_rows]
        mask_rows = same_sentence[first_row : first_row + block_rows][None]
        scores = (
            jnp.einsum("qhd,khd->hqk", rows_query, key_heads, preferred_element_type=jnp.float32)
            * score_scale
        )
        scores = jnp.where(mask_rows, scores, -1000000000.0)
        attn_probs = jnp.exp(scores - log_totals[:, first_row : first_row + block_rows])
        prob_grad = jnp.einsum(
            "qhd,khd->hqk", rows_grad, value_heads, preferred_element_type=jnp.float32
        )
        diag_term = jnp.sum(attn_probs * prob_grad, axis=-1, keepdims=True)
        score_grad = jnp.where(mask_rows, attn_probs * (prob_grad - diag_term), 0.0).astype(
            jnp.bfloat16
        )
        query_parts.append(
            jnp.einsum("hqk,khd->qhd", score_grad, key_heads, preferred_element_type=jnp.float32)
            * score_scale
        )
        key_grad = (
            key_grad
            + jnp.einsum("hqk,qhd->khd", score_grad, rows_query, preferred_element_type=jnp.float32)
            * score_scale
        )
        value_grad = value_grad + jnp.einsum(
            "hqk,qhd->khd",
            attn_probs.astype(jnp.bfloat16),
            rows_grad,
            preferred_element_type=jnp.float32,
        )
    width = HEADS * HEAD_DIM
    query_grad = jnp.concatenate(query_parts, axis=0).reshape(length, width).astype(jnp.bfloat16)
    return (
        query_grad,
        key_grad.reshape(length, width).astype(jnp.bfloat16),
        value_grad.reshape(length, width).astype(jnp.bfloat16),
    )


def body(
    decoder_input,
    target_embed,
    encoder_states,
    sentence_ids,
    position_ranks,
    hamming_counts,
    output_grad,
    attn_in,
    attn_out,
    ffn_in,
    ffn_out,
    small_params,
    attn_in_mom,
    attn_out_mom,
    ffn_in_mom,
    ffn_out_mom,
    small_mom,
    attn_in_err,
    attn_out_err,
    ffn_in_err,
    ffn_out_err,
    attn_in_fac,
    attn_out_fac,
    ffn_in_fac,
    ffn_out_fac,
    attn_in_avg,
    attn_out_avg,
    ffn_in_avg,
    ffn_out_avg,
    small_avg,
):
    whole_in, whole_out, whole_first, whole_second, whole_small = (
        lax.all_gather(attn_in.astype(jnp.bfloat16), "wide", axis=1, tiled=True),
        lax.all_gather(attn_out.astype(jnp.bfloat16), "wide", axis=1, tiled=True),
        lax.all_gather(ffn_in.astype(jnp.bfloat16), "wide", axis=1, tiled=True),
        lax.all_gather(ffn_out.astype(jnp.bfloat16), "wide", axis=1, tiled=True),
        lax.all_gather(small_params.astype(jnp.bfloat16), "wide", axis=1, tiled=True),
    )
    small_full = whole_small.astype(jnp.float32)
    sentence = sentence_ids[0]
    same_sentence = sentence[:, None] == sentence[None, :]
    labels = lax.broadcasted_iota(jnp.int32, (1, hamming_counts.shape[1]), 1)
    per_pos = jnp.sum(jnp.where(sentence[:, None] == labels, hamming_counts[0][None, :], 0), axis=1)
    glance = 2 * position_ranks[0] < per_pos
    mixed_in = jnp.where(glance[:, None], target_embed[0], decoder_input[0])
    encoder = encoder_states[0]
    length = mixed_in.shape[0]
    model_width = mixed_in.shape[1]
    query_one, keys_one, values_one, mixed_one, totals_one = attend_forward(
        mixed_in, mixed_in, whole_in[0], whole_in[1], whole_in[2], same_sentence
    )
    resid_one = mixed_in.astype(jnp.float32) + matmul(mixed_one, whole_out[0])
    hidden_one, normed_one, inv_one = layer_norm(resid_one, small_full[0], small_full[1])
    hidden_one_low = hidden_one.astype(jnp.bfloat16)
    query_two, keys_two, values_two, mixed_two, totals_two = attend_forward(
        hidden_one_low, encoder, whole_in[3], whole_in[4], whole_in[5], same_sentence
    )
    resid_two = hidden_one + matmul(mixed_two, whole_out[1])
    hidden_two, normed_two, inv_two = layer_norm(resid_two, small_full[2], small_full[3])
    hidden_two_low = hidden_two.astype(jnp.bfloat16)
    inner_pre = matmul(hidden_two_low, whole_first[0]) + small_full[7:].reshape(-1)
    act_out = gelu_exact(inner_pre).astype(jnp.bfloat16)
    resid_three = hidden_two + (matmul(act_out, whole_second[0]) + small_full[6])
    layer_out, normed_three, inv_three = layer_norm(resid_three, small_full[4], small_full[5])
    upstream = output_grad[0].astype(jnp.float32)
    grad_three, gain_three, shift_three = layer_norm_back(
        upstream, small_full[4], normed_three, inv_three
    )
    branch_grad = grad_three.astype(jnp.bfloat16)
    second_grad = contract_rows(act_out, branch_grad)
    bias_out_grad = jnp.sum(branch_grad.astype(jnp.float32), axis=0)
    inner_grad = (times_transpose(branch_grad, whole_second[0]) * gelu_slope(inner_pre)).astype(
        jnp.bfloat16
    )
    bias_in_grad = jnp.sum(inner_grad.astype(jnp.float32), axis=0)
    first_grad = contract_rows(hidden_two_low, inner_grad)
    hidden_two_grad = grad_three + times_transpose(inner_grad, whole_first[0])
    grad_two, gain_two, shift_two = layer_norm_back(
        hidden_two_grad, small_full[2], normed_two, inv_two
    )
    out_two_in = grad_two.astype(jnp.bfloat16)
    out_two_grad = contract_rows(mixed_two, out_two_in)
    mixed_two_grad = times_transpose(out_two_in, whole_out[1]).astype(jnp.bfloat16)
    query_grad_two, key_grad_two, value_grad_two = attend_backward(
        mixed_two_grad, query_two, keys_two, values_two, totals_two, same_sentence
    )
    hidden_one_grad = grad_two + times_transpose(query_grad_two, whole_in[3])
    grad_one, gain_one, shift_one = layer_norm_back(
        hidden_one_grad, small_full[0], normed_one, inv_one
    )
    out_one_in = grad_one.astype(jnp.bfloat16)
    out_one_grad = contract_rows(mixed_one, out_one_in)
    mixed_one_grad = times_transpose(out_one_in, whole_out[0]).astype(jnp.bfloat16)
    query_grad_one, key_grad_one, value_grad_one = attend_backward(
        mixed_one_grad, query_one, keys_one, values_one, totals_one, same_sentence
    )
    input_grad = (
        grad_one
        + times_transpose(query_grad_one, whole_in[0])
        + times_transpose(key_grad_one, whole_in[1])
        + times_transpose(value_grad_one, whole_in[2])
    )
    attn_in_grad = jnp.stack(
        [
            contract_rows(mixed_in, query_grad_one),
            contract_rows(mixed_in, key_grad_one),
            contract_rows(mixed_in, value_grad_one),
            contract_rows(hidden_one_low, query_grad_two),
            contract_rows(encoder, key_grad_two),
            contract_rows(encoder, value_grad_two),
        ]
    )
    attn_out_grad = jnp.stack([out_one_grad, out_two_grad])
    small_grad = jnp.concatenate(
        [
            jnp.stack(
                [gain_one, shift_one, gain_two, shift_two, gain_three, shift_three, bias_out_grad]
            ),
            bias_in_grad.reshape(-1, model_width),
        ],
        axis=0,
    )
    shards = (
        lax.psum_scatter(attn_in_grad, "wide", scatter_dimension=1, tiled=True),
        lax.psum_scatter(attn_out_grad, "wide", scatter_dimension=1, tiled=True),
        lax.psum_scatter(first_grad[None], "wide", scatter_dimension=1, tiled=True),
        lax.psum_scatter(second_grad[None], "wide", scatter_dimension=1, tiled=True),
        lax.psum_scatter(small_grad, "wide", scatter_dimension=1, tiled=True),
    )
    scaling = (length * lax.axis_size("wide")) ** (-0.5)
    replicas = lax.axis_size("rep")
    fulls, lefts = ([], [])
    for gradient, error, factor_in in zip(
        shards[:4],
        (attn_in_err, attn_out_err, ffn_in_err, ffn_out_err),
        (attn_in_fac, attn_out_fac, ffn_in_fac, ffn_out_fac),
    ):
        full_grad = gradient * scaling + error[0]
        fulls.append(full_grad)
        lefts.append(jnp.einsum("knm,kmq->knq", full_grad, factor_in, precision=FULL_PRECISION))
    summed = lax.psum((lefts[0], lefts[1], lefts[2], lefts[3], shards[4] * scaling), "rep")
    left_mean = [piece / replicas for piece in summed[:4]]
    local_grams = [
        jnp.einsum("knq,kns->kqs", piece, piece, precision=FULL_PRECISION) for piece in left_mean
    ]
    grams = lax.psum((local_grams[0], local_grams[1], local_grams[2], local_grams[3]), "wide")
    orthos, rights = ([], [])
    for full_grad, piece, gram in zip(fulls, left_mean, grams):
        cholesky_factor = jnp.linalg.cholesky(gram)
        orthonormal = jnp.swapaxes(
            jax.scipy.linalg.solve_triangular(
                cholesky_factor, jnp.swapaxes(piece, 1, 2), lower=True
            ),
            1,
            2,
        )
        orthos.append(orthonormal)
        rights.append(jnp.einsum("knm,knq->kmq", full_grad, orthonormal, precision=FULL_PRECISION))
    right_sums = lax.psum((rights[0], rights[1], rights[2], rights[3]), ("rep", "wide"))
    reduced, new_errors, new_factors = ([], [], [])
    for full_grad, orthonormal, right_sum in zip(fulls, orthos, right_sums):
        right_mean = right_sum / replicas
        approx = jnp.einsum("knq,kmq->knm", orthonormal, right_mean, precision=FULL_PRECISION)
        reduced.append(approx)
        new_errors.append((full_grad - approx)[None])
        new_factors.append(right_mean)
    reduced.append(summed[4] / replicas)
    masters = (attn_in, attn_out, ffn_in, ffn_out, small_params)
    momenta = (attn_in_mom, attn_out_mom, ffn_in_mom, ffn_out_mom, small_mom)
    averages = (attn_in_avg, attn_out_avg, ffn_in_avg, ffn_out_avg, small_avg)
    rates = (LEARN_RATE, LEARN_RATE, LEARN_RATE, LEARN_RATE, VECTOR_RATE)
    new_weights, new_momenta, new_averages = ([], [], [])
    for master, moment, average, update, rate in zip(masters, momenta, averages, reduced, rates):
        moment_new = MOMENTUM * moment + update
        weight_new = master - rate * moment_new
        new_weights.append(weight_new)
        new_momenta.append(moment_new)
        new_averages.append(average + AVERAGE * (weight_new - average))
    return (
        layer_out.astype(jnp.bfloat16)[None],
        input_grad[None],
        new_weights[0],
        new_weights[1],
        new_weights[2],
        new_weights[3],
        new_weights[4],
        new_momenta[0],
        new_momenta[1],
        new_momenta[2],
        new_momenta[3],
        new_momenta[4],
        new_errors[0],
        new_errors[1],
        new_errors[2],
        new_errors[3],
        new_factors[0],
        new_factors[1],
        new_factors[2],
        new_factors[3],
        new_averages[0],
        new_averages[1],
        new_averages[2],
        new_averages[3],
        new_averages[4],
    )


def solution(mesh):
    placed = (
        P(("rep", "wide"), None, None),
        P(("rep", "wide"), None, None),
        P(("rep", "wide"), None, None),
        P(("rep", "wide"), None),
        P(("rep", "wide"), None),
        P(("rep", "wide"), None),
        P(("rep", "wide"), None, None),
        P(None, "wide", None),
        P(None, "wide", None),
        P(None, "wide", None),
        P(None, "wide", None),
        P(None, "wide"),
        P(None, "wide", None),
        P(None, "wide", None),
        P(None, "wide", None),
        P(None, "wide", None),
        P(None, "wide"),
        P("rep", None, "wide", None),
        P("rep", None, "wide", None),
        P("rep", None, "wide", None),
        P("rep", None, "wide", None),
        P(),
        P(),
        P(),
        P(),
        P(None, "wide", None),
        P(None, "wide", None),
        P(None, "wide", None),
        P(None, "wide", None),
        P(None, "wide"),
    )
    return jax.shard_map(
        body,
        mesh=mesh,
        in_specs=placed,
        out_specs=(
            P(("rep", "wide"), None, None),
            P(("rep", "wide"), None, None),
            P(None, "wide", None),
            P(None, "wide", None),
            P(None, "wide", None),
            P(None, "wide", None),
            P(None, "wide"),
            P(None, "wide", None),
            P(None, "wide", None),
            P(None, "wide", None),
            P(None, "wide", None),
            P(None, "wide"),
            P("rep", None, "wide", None),
            P("rep", None, "wide", None),
            P("rep", None, "wide", None),
            P("rep", None, "wide", None),
            P(),
            P(),
            P(),
            P(),
            P(None, "wide", None),
            P(None, "wide", None),
            P(None, "wide", None),
            P(None, "wide", None),
            P(None, "wide"),
        ),
        check_vma=False,
    )
```

profile of v0, /device:TPU:8, one launch (start us, length us, event | category | flops | bytes accessed | tf_op | source)
XLA Modules:
  0.0 850.5 jit_solution(8330408472760638968)
XLA Ops:
  15.6 14.4 %all-gather = bf16[8,64,11]{1,2,0:T(8,128)(2,1)S(1)} all-gather(bf16[1,64,11]{1,2,0:T(8,128)(2,1)S(1)} %convert_bitcast_fusion.1), channel_id=1, replica_groups=mesh['rep'=4,'wide'=8] {'wide'}, dimensions={0}, use_global_device_ids=true | all-gather | bytes 12672 | tf_op jit(solution)/shard_map/all_gather | solution.py:182
  42.6 6.3 all-gather.6.cloned.1.call-done
  56.9 3.5 fusion.16
  63.2 4.5 fusion.147
  70.9 4.0 fusion.17
  77.6 4.5 fusion.146
  90.2 7.8 fusion.257
  98.1 3.5 fusion.19
  102.4 3.8 fusion.144
  106.2 7.9 fusion.18
  114.1 7.6 fusion.145
  123.1 8.0 multiply_convert_fusion
  131.1 3.7 all-gather.12.cloned.1.call-done
  134.8 6.2 fusion.259
  144.2 7.0 convert_reduce_fusion
  151.2 7.2 multiply_reduce_fusion.4
  161.7 8.2 fusion.264
  169.9 8.2 fusion.265
  178.1 29.8 %fusion.141 = bf16[8,64,512]{2,1,0:T(8,128)(2,1)} fusion(bf16[1024,8,64]{0,2,1:T(8,128)(2,1)} %bitcast.457, f32[8,512,1024]{2,1,0:T(8,128)} %fusion.264, f32[8,512,1024]{2,1,0:T(8,128)} %get-tuple-element.223, f32[8,512]{1,0:T(8,128)S(1)} %log_add_fusion.3, pred[512,1024]{1,0:T(8,128)(4,1)} %copy-done.20), kind=kOutput, calls=%fused_computation.165 | convolution fusion | flops 566760448 | bytes 35667968 | tf_op jit(solution)/shard_map/hqk,khd->qhd/dot_general | solution.py:122
  207.9 30.3 %fusion.132 = bf16[8,64,512]{2,1,0:T(8,128)(2,1)} fusion(bf16[1024,8,64]{0,2,1:T(8,128)(2,1)} %bitcast.458, f32[8,512,1024]{2,1,0:T(8,128)} %fusion.265, f32[8,512,1024]{2,1,0:T(8,128)} %copy-done.3, f32[8,512]{1,0:T(8,128)S(1)} %log_add_fusion.2, pred[512,1024]{1,0:T(8,128)(4,1)} %copy-done.21), kind=kOutput, calls=%fused_computation.162 | convolution fusion | flops 566760448 | bytes 35667968 | tf_op jit(solution)/shard_map/hqk,khd->qhd/dot_general | solution.py:122
  238.2 4.6 multiply_reduce_fusion.5
  250.5 6.9 convolution_bitcast_fusion
  260.4 7.3 convolution_bitcast_fusion.1
  270.1 9.5 %fusion.266 = f32[8,512,1024]{2,1,0:T(8,128)} fusion(bf16[512,8,64]{0,2,1:T(8,128)(2,1)} %bitcast.443, bf16[1024,8,64]{0,2,1:T(8,128)(2,1)} %bitcast.433), kind=kOutput, calls=%fused_computation.369 | convolution fusion | flops 536870912 | bytes 18350080 | tf_op jit(solution)/shard_map/qhd,khd->hqk/dot_general | solution.py:114
  279.5 30.4 %fusion.135 = bf16[8,64,512]{2,1,0:T(8,128)(2,1)} fusion(bf16[1024,8,64]{0,2,1:T(8,128)(2,1)} %bitcast.453, f32[8,512,1024]{2,1,0:T(8,128)} %fusion.266, f32[8,512,1024]{2,1,0:T(8,128)} %copy-done.1, f32[8,512]{1,0:T(8,128)S(1)} %log_add_fusion.1, pred[512,1024]{1,0:T(8,128)(4,1)} %copy-done.20), kind=kOutput, calls=%fused_computation.163 | convolution fusion | flops 566760448 | bytes 35667968 | tf_op jit(solution)/shard_map/hqk,khd->qhd/dot_general | solution.py:122
  309.9 9.7 %fusion.267 = f32[8,512,1024]{2,1,0:T(8,128)} fusion(bf16[512,8,64]{0,2,1:T(8,128)(2,1)} %bitcast.445, bf16[1024,8,64]{0,2,1:T(8,128)(2,1)} %bitcast.434), kind=kOutput, calls=%fused_computation.370 | convolution fusion | flops 536870912 | bytes 18350080 | tf_op jit(solution)/shard_map/qhd,khd->hqk/dot_general | solution.py:114
  319.6 30.3 %fusion.138 = bf16[8,64,512]{2,1,0:T(8,128)(2,1)} fusion(bf16[1024,8,64]{0,2,1:T(8,128)(2,1)} %bitcast.454, f32[8,512,1024]{2,1,0:T(8,128)} %fusion.267, f32[8,512,1024]{2,1,0:T(8,128)} %copy-done.2, f32[8,512]{1,0:T(8,128)S(1)} %log_add_fusion, pred[512,1024]{1,0:T(8,128)(4,1)} %copy-done.21), kind=kOutput, calls=%fused_computation.164 | convolution fusion | flops 566760448 | bytes 35667968 | tf_op jit(solution)/shard_map/hqk,khd->qhd/dot_general | solution.py:122
  350.0 3.3 fusion.119
  353.3 31.7 %fusion.45 = f32[8,64,1024]{2,1,0:T(8,128)} fusion(bf16[512,8,64]{0,2,1:T(8,128)(2,1)} %bitcast.466, f32[8,512,1024]{2,1,0:T(8,128)} %fusion.265, f32[8,512,1024]{2,1,0:T(8,128)} %copy-done.3, f32[8,512]{1,0:T(8,128)S(1)} %log_add_fusion.2, pred[512,1024]{1,0:T(8,128)(4,1)} %copy-done.21), kind=kOutput, calls=%fused_computation.58 | convolution fusion | flops 566236160 | bytes 36716544 | tf_op jit(solution)/shard_map/hqk,qhd->khd/dot_general | solution.py:127
  385.0 31.8 %fusion.51 = f32[8,64,1024]{2,1,0:T(8,128)} fusion(bf16[512,8,64]{0,2,1:T(8,128)(2,1)} %bitcast.462, f32[8,512,1024]{2,1,0:T(8,128)} %fusion.266, f32[8,512,1024]{2,1,0:T(8,128)} %copy-done.1, f32[8,512]{1,0:T(8,128)S(1)} %log_add_fusion.1, pred[512,1024]{1,0:T(8,128)(4,1)} %copy-done.20), kind=kOutput, calls=%fused_computation.60 | convolution fusion | flops 566236160 | bytes 36716544 | tf_op jit(solution)/shard_map/hqk,qhd->khd/dot_general | solution.py:127
  416.7 31.8 %multiply_convert_fusion.2 = bf16[8,64,1024]{2,1,0:T(8,128)(2,1)} fusion(f32[8,64,1024]{2,1,0:T(8,128)} %fusion.51, bf16[512,8,64]{0,2,1:T(8,128)(2,1)} %bitcast.460, f32[8,512,1024]{2,1,0:T(8,128)} %fusion.267, f32[8,512,1024]{2,1,0:T(8,128)} %copy-done.2, f32[8,512]{1,0:T(8,128)S(1)} %log_add_fusion, pred[512,1024]{1,0:T(8,128)(4,1)} %copy-done.21), kind=kOutput, calls=%fused_computation.112 | convolution fusion | flops 567809024 | bytes 37765120 | tf_op jit(solution)/shard_map/hqk,qhd->khd/dot_general | solution.py:127
  448.5 3.3 fusion.118
  451.9 7.5 fusion.30
  459.4 7.7 add_convert_fusion.1
  469.8 32.2 %multiply_convert_fusion.1 = bf16[8,64,1024]{2,1,0:T(8,128)(2,1)} fusion(f32[8,64,1024]{2,1,0:T(8,128)} %fusion.45, bf16[512,8,64]{0,2,1:T(8,128)(2,1)} %bitcast.464, f32[8,512,1024]{2,1,0:T(8,128)} %fusion.264, f32[8,512,1024]{2,1,0:T(8,128)} %get-tuple-element.223, f32[8,512]{1,0:T(8,128)S(1)} %log_add_fusion.3, pred[512,1024]{1,0:T(8,128)(4,1)} %copy-done.20), kind=kOutput, calls=%fused_computation.109 | convolution fusion | flops 567809024 | bytes 37765120 | tf_op jit(solution)/shard_map/hqk,qhd->khd/dot_general | solution.py:127
  501.9 3.7 fusion.116
  508.6 7.3 fusion.34
  515.9 7.6 add_convert_fusion
  546.5 45.5 %reduce-scatter.8.cloned.1.call-done = f32[6,64,512]{2,1,0:T(8,128)} async-done(((f32[6,512,512]{2,1,0:T(8,128)}), f32[6,64,512]{2,1,0:T(8,128)}) %reduce-scatter.8.cloned.1.call-update) | async-done | bytes 786448 | tf_op jit(solution)/shard_map/reduce_scatter | solution.py:269
  594.0 18.4 %all-reduce.3 = (f32[6,64,8]{1,2,0:T(8,128)S(1)}, f32[1,64,8]{1,2,0:T(8,128)S(1)}, f32[2,64,8]{1,2,0:T(8,128)S(1)}, f32[1,256,8]{1,2,0:T(8,128)S(1)}, f32[11,64]{1,0:T(8,128)}) all-reduce(f32[6,64,8]{1,2,0:T(8,128)S(1)} %fusion.241, f32[1,64,8]{1,2,0:T(8,128)} %convolution_bitcast_fusion.17, ...), channel_id=1, replica_groups=mesh['rep'=4,'wide'=8] {'rep'}, use_global_device_ids=true, to_apply=%region_26.27 | all-reduce | flops 7360 | bytes 58880 | tf_op jit(solution)/shard_map/psum | solution.py:286
  613.2 25.4 %all-reduce.2 = (f32[6,8,8]{1,2,0:T(8,128)S(1)}, f32[1,8,8]{1,2,0:T(8,128)S(1)}, f32[2,8,8]{1,2,0:T(8,128)S(1)}, f32[1,8,8]{1,2,0:T(8,128)S(1)}) all-reduce(f32[6,8,8]{1,2,0:T(8,128)S(1)} %fusion.185, f32[1,8,8]{1,2,0:T(8,128)S(1)} %convolution_bitcast_fusion.16, ...), channel_id=1, replica_groups=mesh['rep'=4,'wide'=8] {'wide'}, use_global_device_ids=true, to_apply=%region_27.28 | all-reduce | flops 640 | bytes 5120 | tf_op jit(solution)/shard_map/psum | solution.py:291
  650.6 4.4 custom-call.27
  656.6 3.7 custom-call.28
  662.4 42.2 %all-reduce = (f32[2,512,8]{1,2,0:T(8,128)S(1)}, f32[1,512,8]{1,2,0:T(8,128)S(1)}) all-reduce(f32[2,512,8]{1,2,0:T(8,128)S(1)} %fusion.238, f32[1,512,8]{1,2,0:T(8,128)S(1)} %convolution_bitcast_fusion.13), channel_id=1, replica_groups=mesh['rep'=4,'wide'=8] {'rep','wide'}, use_global_device_ids=true, to_apply=%region_36.37 | all-reduce | flops 12288 | bytes 98304 | tf_op jit(solution)/shard_map/psum | solution.py:304
  711.8 3.6 multiply_add_fusion.4
  716.8 116.8 %all-reduce.6.cloned.1.call-done = (f32[6,512,8]{1,2,0:T(8,128)}, f32[1,2048,8]{1,2,0:T(8,128)}) async-done(((f32[6,512,8]{1,2,0:T(8,128)}, f32[1,2048,8]{1,2,0:T(8,128)}), (f32[6,512,8]{1,2,0:T(8,128)}, f32[1,2048,8]{1,2,0:T(8,128)})) %all-reduce.6.cloned.1.call-update) | async-done | bytes 163856 | tf_op jit(solution)/shard_map/psum | solution.py:304
  835.4 3.8 multiply_add_fusion.5
  839.2 4.3 multiply_add_fusion.2
  (299 shorter events, 123.9 us)
Async XLA Ops:
  7.2 79.0 %copy-start = (bf16[1,1024,512]{2,1,0:T(8,128)(2,1)S(1)}, bf16[1,1024,512]{2,1,0:T(8,128)(2,1)}, u32[]{:S(2)}) copy-start(bf16[1,1024,512]{2,1,0:T(8,128)(2,1)} %param.33) | copy-start | bytes 3145732
  7.2 30.4 %copy-start.26 = (bf16[1,1024,512]{2,1,0:T(8,128)(2,1)S(1)}, bf16[1,1024,512]{2,1,0:T(8,128)(2,1)}, u32[]{:S(2)}) copy-start(bf16[1,1024,512]{2,1,0:T(8,128)(2,1)} %param.31) | copy-start | bytes 3145732
  7.2 29.0 %copy-start.25 = (bf16[1,1024,512]{2,1,0:T(8,128)(2,1)S(1)}, bf16[1,1024,512]{2,1,0:T(8,128)(2,1)}, u32[]{:S(2)}) copy-start(bf16[1,1024,512]{2,1,0:T(8,128)(2,1)} %param.32) | copy-start | bytes 3145732
  7.2 41.7 %all-gather.6.cloned.1.call-start = ((), (), s32[]{:S(2)}) async-start(), calls=%async_computation.5 | async-start | bytes 3538944 | tf_op jit(solution)/shard_map/all_gather | solution.py:178
  9.4 72.6 %all-gather.8.cloned.1.call-start = ((), (), s32[]{:S(2)}) async-start(), calls=%async_computation.6 | async-start | bytes 1179648 | tf_op jit(solution)/shard_map/all_gather | solution.py:179
  11.1 112.0 %all-gather.10.cloned.1.call-start = ((), (), s32[]{:S(2)}) async-start(), calls=%async_computation.7 | async-start | bytes 2359296 | tf_op jit(solution)/shard_map/all_gather | solution.py:180
  13.0 121.8 %all-gather.12.cloned.1.call-start = ((), (), s32[]{:S(2)}) async-start(), calls=%async_computation.8 | async-start | bytes 2359296 | tf_op jit(solution)/shard_map/all_gather | solution.py:181
  14.8 524.8 %reduce-scatter.16.cloned.1.call-start = ((), (), s32[]{:S(2)}) async-start(), calls=%async_computation.13 | async-start | bytes 294912
  30.1 91.7 %copy-start.67 = (f32[1,512]{1,0:T(1,128)}, f32[1,512]{1,0:T(1,128)S(1)}, u32[]{:S(2)}) copy-start(f32[1,512]{1,0:T(1,128)S(1)} %get-tuple-element.212) | copy-start | bytes 6148
  40.4 16.5 %copy-start.4 = (bf16[1,1024,512]{1,2,0:T(8,128)(2,1)}, bf16[1,1024,512]{1,2,0:T(8,128)(2,1)S(1)}, u32[]{:S(2)}) copy-start(bf16[1,1024,512]{1,2,0:T(8,128)(2,1)S(1)} %copy.161) | copy-start | bytes 3145732
  42.6 44.4 %copy-start.21 = (pred[512,1024]{1,0:T(8,128)(4,1)}, pred[512,1024]{1,0:T(8,128)(4,1)S(1)}, u32[]{:S(2)}) copy-start(pred[512,1024]{1,0:T(8,128)(4,1)S(1)} %get-tuple-element.200) | copy-start | bytes 1572868
  42.6 47.6 %copy-start.20 = (pred[512,1024]{1,0:T(8,128)(4,1)}, pred[512,1024]{1,0:T(8,128)(4,1)S(1)}, u32[]{:S(2)}) copy-start(pred[512,1024]{1,0:T(8,128)(4,1)S(1)} %get-tuple-element.199) | copy-start | bytes 1572868
  51.1 16.5 %copy-start.32 = (bf16[512,512]{0,1:T(8,128)(2,1)}, bf16[512,512]{0,1:T(8,128)(2,1)S(1)}, u32[]{:S(2)}) copy-start(bf16[512,512]{0,1:T(8,128)(2,1)S(1)} %get-tuple-element.202) | copy-start | bytes 1572868
  53.6 14.0 %copy-start.28 = (bf16[1024,512]{0,1:T(8,128)(2,1)}, bf16[1024,512]{0,1:T(8,128)(2,1)S(1)}, u32[]{:S(2)}) copy-start(bf16[1024,512]{0,1:T(8,128)(2,1)S(1)} %convolution_convert_fusion.5) | copy-start | bytes 3145732
  62.7 12.2 %copy-start.6 = (bf16[1024,512]{0,1:T(8,128)(2,1)}, bf16[1024,512]{0,1:T(8,128)(2,1)S(1)}, u32[]{:S(2)}) copy-start(bf16[1024,512]{0,1:T(8,128)(2,1)S(1)} %convolution_convert_fusion.7) | copy-start | bytes 3145732
  84.9 36.9 %copy-start.9 = (f32[1024,512]{0,1:T(8,128)}, f32[1024,512]{0,1:T(8,128)S(1)}, u32[]{:S(2)}) copy-start(f32[1024,512]{0,1:T(8,128)S(1)} %get-tuple-element.219) | copy-start | bytes 6291460
  90.2 12.2 %copy-start.3 = (f32[8,512,1024]{2,1,0:T(8,128)}, f32[8,512,1024]{2,1,0:T(8,128)S(1)}, u32[]{:S(2)}) copy-start(f32[8,512,1024]{2,1,0:T(8,128)S(1)} %get-tuple-element.221) | copy-start | bytes 50331652
  102.3 11.8 %copy-start.7 = (bf16[1024,512]{0,1:T(8,128)(2,1)}, bf16[1024,512]{0,1:T(8,128)(2,1)S(1)}, u32[]{:S(2)}) copy-start(bf16[1024,512]{0,1:T(8,128)(2,1)S(1)} %convolution_convert_fusion.4) | copy-start | bytes 3145732
  106.2 15.6 %copy-start.43 = (bf16[8,64,512]{2,1,0:T(8,128)(2,1)}, bf16[8,64,512]{2,1,0:T(8,128)(2,1)S(1)}, u32[]{:S(2)}) copy-start(bf16[8,64,512]{2,1,0:T(8,128)(2,1)S(1)} %fusion.144) | copy-start | bytes 1572868
  114.1 7.7 copy-start.37
  122.7 8.4 copy-start.10
  134.8 9.3 %slice-start = ((s8[8388608]{0:T(1024)(128)(4,1)}), s8[4194304]{0:T(1024)(128)(4,1)S(1)}, s32[]{:S(2)}) async-start(s8[8388608]{0:T(1024)(128)(4,1)} %bitcast.526), calls=%async_computation.15 | async-start | bytes 8388608
  134.8 9.3 %slice-start.1 = ((s8[8388608]{0:T(1024)(128)(4,1)}), s8[4194304]{0:T(1024)(128)(4,1)S(1)}, s32[]{:S(2)}) async-start(s8[8388608]{0:T(1024)(128)(4,1)} %bitcast.526), calls=%async_computation.16 | async-start | bytes 8388608
  161.7 8.2 copy-start.12
  161.7 8.2 copy-start.14
  243.8 297.3 %reduce-scatter.10.cloned.1.call-start = ((), (), s32[]{:S(2)}) async-start(), calls=%async_computation.10 | async-start | bytes 2359296 | tf_op jit(solution)/shard_map/reduce_scatter | solution.py:270
  250.4 292.0 %reduce-scatter.14.cloned.1.call-start = ((), (), s32[]{:S(2)}) async-start(), calls=%async_computation.12 | async-start | bytes 4718592 | tf_op jit(solution)/shard_map/reduce_scatter | solution.py:272
  257.5 286.7 %reduce-scatter.12.cloned.1.call-start = ((), (), s32[]{:S(2)}) async-start(), calls=%async_computation.11 | async-start | bytes 4718592 | tf_op jit(solution)/shard_map/reduce_scatter | solution.py:271
  267.7 324.3 %reduce-scatter.8.cloned.1.call-start = ((), (), s32[]{:S(2)}) async-start(), calls=%async_computation.9 | async-start | bytes 7077888 | tf_op jit(solution)/shard_map/reduce_scatter | solution.py:269
  451.9 7.5 copy-start.16
  459.3 8.7 %copy-start.40 = (bf16[1,1024,512]{2,1,0:T(8,128)(2,1)S(1)}, bf16[1,1024,512]{2,1,0:T(8,128)(2,1)}, u32[]{:S(2)}) copy-start(bf16[1,1024,512]{2,1,0:T(8,128)(2,1)} %broadcast_select_fusion) | copy-start | bytes 3145732
  469.8 32.2 %copy-start.68 = (f32[1,512]{1,0:T(1,128)S(1)}, f32[1,512]{1,0:T(1,128)}, u32[]{:S(2)}) copy-start(f32[1,512]{1,0:T(1,128)} %copy-done.67) | copy-start | bytes 6148
  525.3 308.3 %all-reduce.6.cloned.1.call-start = ((), (), s32[]{:S(2)}) async-start(), calls=%async_computation.14 | async-start | bytes 327680 | tf_op jit(solution)/shard_map/psum | solution.py:304
  533.3 7.8 copy-start.30
  533.3 9.2 %copy-start.62 = (f32[1,512,8]{1,2,0:T(8,128)S(1)}, f32[1,512,8]{1,2,0:T(8,128)}, u32[]{:S(2)}) copy-start(f32[1,512,8]{1,2,0:T(8,128)} %param.55) | copy-start | bytes 49156
  533.3 58.8 %copy-start.54 = (f32[6,512,8]{1,2,0:T(8,128)S(1)}, f32[6,512,8]{1,2,0:T(8,128)}, u32[]{:S(2)}) copy-start(f32[6,512,8]{1,2,0:T(8,128)} %param.52) | copy-start | bytes 294916
  536.6 55.5 %copy-start.17 = (f32[1,6,64,512]{3,2,1,0:T(8,128)S(1)}, f32[1,6,64,512]{3,2,1,0:T(8,128)}, u32[]{:S(2)}) copy-start(f32[1,6,64,512]{3,2,1,0:T(8,128)} %param.48) | copy-start | bytes 2359300
  536.6 124.1 %copy-start.19 = (f32[1,1,256,512]{3,2,1,0:T(8,128)S(1)}, f32[1,1,256,512]{3,2,1,0:T(8,128)}, u32[]{:S(2)}) copy-start(f32[1,1,256,512]{3,2,1,0:T(8,128)} %param.51) | copy-start | bytes 1572868
  536.6 168.1 %copy-start.22 = (f32[1,1,64,2048]{3,2,1,0:T(8,128)S(1)}, f32[1,1,64,2048]{3,2,1,0:T(8,128)}, u32[]{:S(2)}) copy-start(f32[1,1,64,2048]{3,2,1,0:T(8,128)} %param.50) | copy-start | bytes 1572868
  541.1 121.0 %copy-start.31 = (f32[2,64,512]{2,1,0:T(8,128)S(1)}, f32[2,64,512]{2,1,0:T(8,128)}, u32[]{:S(2)}) copy-start(f32[2,64,512]{2,1,0:T(8,128)} %reduce-scatter.10.cloned.1.call-done) | copy-start | bytes 786436
  612.4 103.0 %copy-start.60 = (f32[11,64]{1,0:T(8,128)S(1)}, f32[11,64]{1,0:T(8,128)}, u32[]{:S(2)}) copy-start(f32[11,64]{1,0:T(8,128)} %param.42) | copy-start | bytes 8452
  612.4 103.0 %copy-start.65 = (f32[11,64]{1,0:T(8,128)S(1)}, f32[11,64]{1,0:T(8,128)}, u32[]{:S(2)}) copy-start(f32[11,64]{1,0:T(8,128)} %param.60) | copy-start | bytes 8452
  650.5 64.9 %copy-start.66 = (f32[11,64]{1,0:T(8,128)S(1)}, f32[11,64]{1,0:T(8,128)}, u32[]{:S(2)}) copy-start(f32[11,64]{1,0:T(8,128)} %get-tuple-element.174) | copy-start | bytes 8452
  704.6 134.5 %copy-start.53 = (f32[2,512,8]{1,2,0:T(8,128)}, f32[2,512,8]{1,2,0:T(8,128)S(1)}, u32[]{:S(2)}) copy-start(f32[2,512,8]{1,2,0:T(8,128)S(1)} %broadcast_multiply_fusion.2) | copy-start | bytes 98308
  704.7 134.5 %copy-start.55 = (f32[1,512,8]{1,2,0:T(8,128)}, f32[1,512,8]{1,2,0:T(8,128)S(1)}, u32[]{:S(2)}) copy-start(f32[1,512,8]{1,2,0:T(8,128)S(1)} %broadcast_multiply_fusion.3) | copy-start | bytes 49156
  709.1 130.1 %copy-start.18 = (f32[6,64,512]{2,1,0:T(8,128)S(1)}, f32[6,64,512]{2,1,0:T(8,128)}, u32[]{:S(2)}) copy-start(f32[6,64,512]{2,1,0:T(8,128)} %reduce-scatter.8.cloned.1.call-done) | copy-start | bytes 2359300
  834.5 9.0 %copy-start.47 = (f32[6,512,8]{1,2,0:T(8,128)}, f32[6,512,8]{1,2,0:T(8,128)S(1)}, u32[]{:S(2)}) copy-start(f32[6,512,8]{1,2,0:T(8,128)S(1)} %broadcast_multiply_fusion) | copy-start | bytes 294916
  835.4 8.1 copy-start.48
  (34 other events, 163.7 us)
Sparse Core Ops, SparseCore 0:
  10.3 38.6 all-gather.5
  51.1 22.2 all-gather.7
  75.6 28.5 all-gather.9
  106.2 28.5 all-gather.11
  243.9 26.3 reduce-scatter.15
  272.5 33.8 reduce-scatter.9
  308.9 48.6 reduce-scatter.13
  359.9 48.1 reduce-scatter.11
  525.4 66.5 reduce-scatter.7
  709.3 124.2 all-reduce.5
where the time goes:
time: 862 us; the launch traced here: 851 us
  matrix products  472 us (55%)
  waiting for transfers between devices  172 us (20%)
  blocking collectives  100 us (12%)
  other arithmetic  69.7 us (8%)
  local copies, waits for them, and re-layouts  19.9 us (2%)
  between operations  15.6 us (2%)
    dot_general x4, matrix products, attend_backward(): jnp.einsum('hqk,qhd->khd', score_grad, rows_query, preferred_element_type...  127 us
    dot_general x4, matrix products, attend_backward(): jnp.einsum('hqk,khd->qhd', score_grad, key_heads, preferred_element_type=...  121 us
    psum x1, waiting for transfers between devices, body(): lax.psum((rights[0], rights[1], rights[2], rights[3]), ('rep', 'wide'))  117 us
    reduce_scatter x1, waiting for transfers between devices, body(): lax.psum_scatter(attn_in_grad, 'wide', scatter_dimension=1, tiled=True)  45.5 us
    psum x1, blocking collectives, body(): lax.psum((rights[0], rights[1], rights[2], rights[3]), ('rep', 'wide'))  42.2 us
    dot_general x4, matrix products, attend_backward(): jnp.einsum('qhd,khd->hqk', rows_grad, value_heads, preferred_element_type...  35.5 us
    dot_general x10, matrix products, contract_rows(): lax.dot_general(left_arr, right_arr, (((0,), (0,)), ((), ())), preferred_...  33.5 us
    dot_general x4, matrix products, attend_backward(): jnp.einsum('hqk,qhd->khd', attn_probs.astype(jnp.bfloat16), rows_grad, pr...  30 us
  transfers between devices with their start and end apart: 10, of which 4 were waited for; matrix products, arithmetic and copies ran while one was open for 48% of the time, Pallas kernels for 0%

commit v1 on v0

v1 whole, which is shorter than its diff:
```python
import jax
import jax.numpy as jnp
from jax import lax
from jax.experimental import pallas as pl
from jax.experimental.pallas import tpu as pltpu
from jax.sharding import PartitionSpec as P

HEADS = 8
HEAD_DIM = 64
BLOCK = 256
SPAN = 128
EPS = 1e-05
BF = jnp.bfloat16
F32 = jnp.float32


FULL_PRECISION = lax.Precision.HIGHEST
MOMENTUM = 0.9
LEARN_RATE = 0.1
VECTOR_RATE = 0.5
AVERAGE = 0.25


def dot(a, b):
    return lax.dot_general(a, b, (((1,), (0,)), ((), ())), preferred_element_type=F32)


def dot_nt(a, b):
    return lax.dot_general(a, b, (((1,), (1,)), ((), ())), preferred_element_type=F32)


def dot_tn(a, b):
    return lax.dot_general(a, b, (((0,), (0,)), ((), ())), preferred_element_type=F32)


def gelu_pair(u):
    half = 0.5 * (1.0 + lax.erf(u * 0.7071067811865476))
    return u * half, half + u * jnp.exp(-0.5 * u * u) * 0.3989422804014327


def wide4(col):
    return jnp.concatenate([col] * 4, axis=1)


def norm_parts(resid):
    center = resid - jnp.mean(resid, axis=-1, keepdims=True)
    inv = lax.rsqrt(jnp.mean(center * center, axis=-1, keepdims=True) + EPS)
    return center * inv, inv


def norm_back(up, gain, normed, inv):
    scaled = up * gain
    return inv * (
        scaled
        - jnp.mean(scaled, axis=-1, keepdims=True)
        - normed * jnp.mean(scaled * normed, axis=-1, keepdims=True)
    )


def window(i, length):
    start = max(0, i * BLOCK - SPAN)
    return start, min(length, (i + 1) * BLOCK + SPAN) - start


def head_masks(rows):
    lane = lax.broadcasted_iota(jnp.int32, (rows, 2 * HEAD_DIM), 1)
    return lane < HEAD_DIM


def split_heads(pair, first):
    zero = jnp.zeros_like(pair)
    return jnp.where(first, pair, zero), jnp.where(first, zero, pair)


def attend(q, k, v_t, o, lse, bias, length):
    for i in range(length // BLOCK):
        start, wide = window(i, length)
        rows, keys = pl.ds(i * BLOCK, BLOCK), pl.ds(start, wide)

        @pl.loop(0, HEADS // 2)
        def _(pair):
            lanes = pl.ds(pl.multiple_of(pair * 128, 128), 128)
            k_pair = k[keys, lanes]
            first = head_masks(BLOCK)
            outs = []
            for which, q_head in enumerate(split_heads(q[rows, lanes], first)):
                s = dot_nt(k_pair, q_head) + bias[i, pl.ds(0, wide), :]
                peak = jnp.max(s, axis=0, keepdims=True)
                e = jnp.exp(s - peak)
                total = jnp.sum(e, axis=0, keepdims=True)
                p = (e * (1.0 / total)).astype(BF)
                head = pl.ds(pl.multiple_of(pair * 128 + which * 64, 64), 64)
                outs.append(dot(v_t[head, keys], p))
                lse[pl.ds(pair * 2 + which, 1), rows] = peak + jnp.log(total)
            o[rows, lanes] = jnp.concatenate(outs, axis=0).T.astype(BF)


def attend_back(q, k, v, k_t, do, lse, bias, dq, dk, dv, length):
    dk[...] = jnp.zeros_like(dk)
    dv[...] = jnp.zeros_like(dv)
    for i in range(length // BLOCK):
        start, wide = window(i, length)
        rows, keys = pl.ds(i * BLOCK, BLOCK), pl.ds(start, wide)

        @pl.loop(0, HEADS // 2)
        def _(pair):
            lanes = pl.ds(pl.multiple_of(pair * 128, 128), 128)
            k_pair, v_pair = k[keys, lanes], v[keys, lanes]
            first = head_masks(BLOCK)
            q_heads = split_heads(q[rows, lanes], first)
            d_heads = split_heads(do[rows, lanes], first)
            dq_t, dk_sum, dv_sum = [], None, None
            for which in range(2):
                s = dot_nt(k_pair, q_heads[which]) + bias[i, pl.ds(0, wide), :]
                p = jnp.exp(s - lse[pl.ds(pair * 2 + which, 1), rows])
                dp = dot_nt(v_pair, d_heads[which])
                diag = jnp.sum(p * dp, axis=0, keepdims=True)
                ds = (p * (dp - diag)).astype(BF)
                head = pl.ds(pl.multiple_of(pair * 128 + which * 64, 64), 64)
                dq_t.append(dot(k_t[head, keys], ds))
                dk_one = dot(ds, q_heads[which])
                dv_one = dot(p.astype(BF), d_heads[which])
                dk_sum = dk_one if dk_sum is None else dk_sum + dk_one
                dv_sum = dv_one if dv_sum is None else dv_sum + dv_one
            dq[rows, lanes] = (jnp.concatenate(dq_t, axis=0).T * HEAD_DIM ** (-0.5)).astype(BF)
            dk[keys, lanes] += dk_sum
            dv[keys, lanes] += dv_sum


def layer_kernel(
    sid, rank, ham, dec, tgt, enc, og,
    wa1, wo1, wa2, wo2, w1, w2, small,
    layer_out, in_grad, g1, g2, go2, ga2, go1, ga1, small_grad,
    x, q1, k1, v1, o1, q2, k2, v2, o2, turn, n1, n2, inv1, inv2,
    hid, du, dz, h2b, slope, da, do, bias, lse1, lse2, col,
):
    length, width = x.shape
    blocks = length // BLOCK
    scale = HEAD_DIM ** (-0.5)
    row = lambda r: small[pl.ds(r, 1), :]

    sent = sid[...]
    per_pos = jnp.zeros_like(sent)
    for s in range(ham.shape[1]):
        per_pos = jnp.where(sent == s, ham[0, s], per_pos)
    glance = jnp.where(2 * rank[...] < per_pos, 1.0, 0.0).astype(F32)
    sent_f = sent.astype(F32)
    col[...] = jnp.broadcast_to(glance, (128, length)).T

    @pl.loop(0, blocks)
    def _(i):
        rows = pl.ds(pl.multiple_of(i * BLOCK, BLOCK), BLOCK)
        x[rows, :] = jnp.where(
            wide4(col[rows, :]) > 0.5, tgt[rows, :].astype(F32), dec[rows, :].astype(F32)
        ).astype(BF)

    col[...] = jnp.broadcast_to(sent_f, (128, length)).T
    for i in range(blocks):
        start, wide = window(i, length)
        keys = col[pl.ds(start, wide), :]
        bias[i, pl.ds(0, wide), :] = jnp.where(
            jnp.concatenate([keys, keys], axis=1) == sent_f[:, i * BLOCK : (i + 1) * BLOCK], 0.0, -1e9
        )

    @pl.loop(0, blocks)
    def _(i):
        rows = pl.ds(pl.multiple_of(i * BLOCK, BLOCK), BLOCK)
        x_blk = x[rows, :]
        q1[rows, :] = dot(x_blk, wa1[:, :width]).astype(BF) * jnp.asarray(scale, BF)
        k1[rows, :] = dot(x_blk, wa1[:, width : 2 * width]).astype(BF)
        v = dot(x_blk, wa1[:, 2 * width :]).astype(BF)
        v1[rows, :] = v
        turn[:, rows] = v.T

    attend(q1, k1, turn, o1, lse1, bias, length)

    @pl.loop(0, blocks)
    def _(i):
        rows = pl.ds(pl.multiple_of(i * BLOCK, BLOCK), BLOCK)
        resid = x[rows, :].astype(F32) + dot(o1[rows, :], wo1[...])
        normed, inv = norm_parts(resid)
        n1[rows, :] = normed
        inv1[rows, :] = jnp.broadcast_to(inv, (BLOCK, 128))
        h1b = (normed * row(0) + row(1)).astype(BF)
        q2[rows, :] = dot(h1b, wa2[:, :width]).astype(BF) * jnp.asarray(scale, BF)
        e_blk = enc[rows, :]
        k2[rows, :] = dot(e_blk, wa2[:, width : 2 * width]).astype(BF)
        v = dot(e_blk, wa2[:, 2 * width :]).astype(BF)
        v2[rows, :] = v
        turn[:, rows] = v.T

    attend(q2, k2, turn, o2, lse2, bias, length)

    small_grad[...] = jnp.zeros_like(small_grad)
    hidden = w1.shape[1]
    step = 512
    parts = hidden // step

    def add_small(r, value):
        small_grad[pl.ds(r, 1), :] += jnp.sum(value, axis=0, keepdims=True)

    @pl.loop(0, blocks)
    def _(i):
        rows = pl.ds(pl.multiple_of(i * BLOCK, BLOCK), BLOCK)
        h1 = n1[rows, :] * row(0) + row(1)
        resid = h1 + dot(o2[rows, :], wo2[...])
        normed2, inv = norm_parts(resid)
        n2[rows, :] = normed2
        inv2[rows, :] = jnp.broadcast_to(inv, (BLOCK, 128))
        h2 = normed2 * row(2) + row(3)
        h2_low = h2.astype(BF)
        h2b[rows, :] = h2_low
        for c in range(parts):
            cols = slice(c * step, (c + 1) * step)
            u = dot(h2_low, w1[:, cols]) + small[pl.ds(7 + c, 1), :]
            act, der = gelu_pair(u)
            hid[rows, cols] = act.astype(BF)
            slope[pl.ds(c * BLOCK, BLOCK), :] = der
        resid3 = h2 + (dot(hid[rows, :], w2[...]) + row(6))
        normed3, inv3 = norm_parts(resid3)
        layer_out[rows, :] = (normed3 * row(4) + row(5)).astype(BF)
        up = og[rows, :].astype(F32)
        add_small(4, up * normed3)
        add_small(5, up)
        dr3 = norm_back(up, row(4), normed3, inv3)
        dz_low = dr3.astype(BF)
        dz[rows, :] = dz_low
        add_small(6, dz_low.astype(F32))
        for c in range(parts):
            cols = slice(c * step, (c + 1) * step)
            d = (dot_nt(dz_low, w2[cols, :]) * slope[pl.ds(c * BLOCK, BLOCK), :]).astype(BF)
            du[rows, cols] = d
            add_small(7 + c, d.astype(F32))
        dh2 = dr3 + dot_nt(du[rows, :], w1[...])
        normed2 = n2[rows, :]
        add_small(2, dh2 * normed2)
        add_small(3, dh2)
        dr2 = norm_back(dh2, row(2), normed2, wide4(inv2[rows, :]))
        in_grad[rows, :] = dr2
        da_low = dr2.astype(BF)
        da[rows, :] = da_low
        do[rows, :] = dot_nt(da_low, wo2[...]).astype(BF)

    @pl.loop(0, hidden // 256)
    def _(c):
        cols = pl.ds(pl.multiple_of(c * 256, 256), 256)
        g2[cols, :] = dot_tn(hid[:, cols], dz[...]).astype(BF)

    @pl.loop(0, width // 128)
    def _(c):
        cols = pl.ds(pl.multiple_of(c * 128, 128), 128)
        g1[cols, :] = dot_tn(h2b[:, cols], du[...]).astype(BF)
        go2[cols, :] = dot_tn(o2[:, cols], da[...]).astype(BF)

    dk, dv = slope, n2
    dqkv = hid

    turn[...] = k2[...].T
    attend_back(q2, k2, v2, turn, do, lse2, bias, dqkv, dk, dv, length)
    dqkv[:, width : 2 * width] = dk[...].astype(BF)
    dqkv[:, 2 * width : 3 * width] = dv[...].astype(BF)

    @pl.loop(0, blocks)
    def _(i):
        rows = pl.ds(pl.multiple_of(i * BLOCK, BLOCK), BLOCK)
        normed = n1[rows, :]
        h2b[rows, :] = (normed * row(0) + row(1)).astype(BF)
        dh1 = in_grad[rows, :] + dot_nt(dqkv[rows, :width], wa2[:, :width])
        add_small(0, dh1 * normed)
        add_small(1, dh1)
        dr1 = norm_back(dh1, row(0), normed, wide4(inv1[rows, :]))
        in_grad[rows, :] = dr1
        da_low = dr1.astype(BF)
        da[rows, :] = da_low
        do[rows, :] = dot_nt(da_low, wo1[...]).astype(BF)

    @pl.loop(0, width // 128)
    def _(c):
        cols = pl.ds(pl.multiple_of(c * 128, 128), 128)
        ga2[cols, :width] = dot_tn(h2b[:, cols], dqkv[:, :width]).astype(BF)
        ga2[cols, width:] = dot_tn(enc[:, cols], dqkv[:, width : 3 * width]).astype(BF)
        go1[cols, :] = dot_tn(o1[:, cols], da[...]).astype(BF)

    turn[...] = k1[...].T
    attend_back(q1, k1, v1, turn, do, lse1, bias, dqkv, dk, dv, length)
    dqkv[:, width : 2 * width] = dk[...].astype(BF)
    dqkv[:, 2 * width : 3 * width] = dv[...].astype(BF)

    @pl.loop(0, width // 128)
    def _(c):
        cols = pl.ds(pl.multiple_of(c * 128, 128), 128)
        ga1[cols, :] = dot_tn(x[:, cols], dqkv[:, : 3 * width]).astype(BF)

    @pl.loop(0, blocks)
    def _(i):
        rows = pl.ds(pl.multiple_of(i * BLOCK, BLOCK), BLOCK)
        in_grad[rows, :] += dot_nt(dqkv[rows, : 3 * width], wa1[...])


def run_layer(sid, rank, ham, dec, tgt, enc, og, wa1, wo1, wa2, wo2, w1, w2, small):
    length, width = dec.shape
    hidden = w1.shape[1]
    sds = jax.ShapeDtypeStruct
    vm = pl.BlockSpec(memory_space=pltpu.VMEM)
    tok_b = pltpu.VMEM((length, width), BF)
    tok_f = pltpu.VMEM((length, width), F32)
    return pl.pallas_call(
        layer_kernel,
        out_shape=(
            sds((length, width), BF),
            sds((length, width), F32),
            sds(w1.shape, BF), sds(w2.shape, BF), sds(wo2.shape, BF), sds(wa2.shape, BF),
            sds(wo1.shape, BF), sds(wa1.shape, BF), sds(small.shape, F32),
        ),
        in_specs=[vm, vm, pl.BlockSpec(memory_space=pltpu.SMEM)] + [vm] * 11,
        out_specs=(vm,) * 9,
        scratch_shapes=[tok_b] * 9
        + [pltpu.VMEM((width, length), BF), tok_f, tok_f]
        + [pltpu.VMEM((length, 128), F32)] * 2
        + [pltpu.VMEM((length, hidden), BF)] * 2
        + [tok_b, tok_b, tok_f, tok_b, tok_b]
        + [pltpu.VMEM((length // BLOCK, 2 * BLOCK, BLOCK), F32)]
        + [pltpu.VMEM((HEADS, length), F32)] * 2
        + [pltpu.VMEM((length, 128), F32)],
        compiler_params=pltpu.CompilerParams(vmem_limit_bytes=63 * 2**20),
        name="layer",
    )(sid, rank, ham, dec, tgt, enc, og, wa1, wo1, wa2, wo2, w1, w2, small)


def body(
    decoder_input,
    target_embed,
    encoder_states,
    sentence_ids,
    position_ranks,
    hamming_counts,
    output_grad,
    attn_in,
    attn_out,
    ffn_in,
    ffn_out,
    small_params,
    attn_in_mom,
    attn_out_mom,
    ffn_in_mom,
    ffn_out_mom,
    small_mom,
    attn_in_err,
    attn_out_err,
    ffn_in_err,
    ffn_out_err,
    attn_in_fac,
    attn_out_fac,
    ffn_in_fac,
    ffn_out_fac,
    attn_in_avg,
    attn_out_avg,
    ffn_in_avg,
    ffn_out_avg,
    small_avg,
):
    small_full = lax.all_gather(
        small_params.astype(BF), "wide", axis=1, tiled=True
    ).astype(F32)

    def columns(stack):
        return jnp.swapaxes(stack, 0, 1).reshape(stack.shape[1], -1)

    def gather(rows):
        return lax.all_gather(rows.astype(BF), "wide", axis=0, tiled=True)

    whole = [
        gather(columns(attn_in[:3])), gather(attn_out[0]),
        gather(columns(attn_in[3:])), gather(attn_out[1]),
        gather(ffn_in[0]), gather(ffn_out[0]),
    ]
    length = decoder_input.shape[1]
    layer_out, input_grad, g1, g2, go2, ga2, go1, ga1, small_grad = run_layer(
        sentence_ids, position_ranks, hamming_counts, decoder_input[0], target_embed[0],
        encoder_states[0], output_grad[0], *whole, small_full
    )

    def scatter(rows):
        return lax.psum_scatter(rows, "wide", scatter_dimension=0, tiled=True).astype(F32)

    def stack_of(rows):
        return jnp.swapaxes(rows.reshape(rows.shape[0], -1, g1.shape[0]), 0, 1)

    second, first = scatter(g2), scatter(g1)
    out_two, in_two, out_one, in_one = scatter(go2), scatter(ga2), scatter(go1), scatter(ga1)
    shards = (
        jnp.concatenate([stack_of(in_one), stack_of(in_two)], axis=0),
        jnp.stack([out_one, out_two]),
        first[None],
        second[None],
        lax.psum_scatter(small_grad, "wide", scatter_dimension=1, tiled=True),
    )
    scaling = (length * lax.axis_size("wide")) ** (-0.5)
    replicas = lax.axis_size("rep")
    fulls, lefts = ([], [])
    for gradient, error, factor_in in zip(
        shards[:4],
        (attn_in_err, attn_out_err, ffn_in_err, ffn_out_err),
        (attn_in_fac, attn_out_fac, ffn_in_fac, ffn_out_fac),
    ):
        full_grad = gradient * scaling + error[0]
        fulls.append(full_grad)
        lefts.append(jnp.einsum("knm,kmq->knq", full_grad, factor_in, precision=FULL_PRECISION))
    summed = lax.psum((lefts[0], lefts[1], lefts[2], lefts[3], shards[4] * scaling), "rep")
    left_mean = [piece / replicas for piece in summed[:4]]
    local_grams = [
        jnp.einsum("knq,kns->kqs", piece, piece, precision=FULL_PRECISION) for piece in left_mean
    ]
    grams = lax.psum((local_grams[0], local_grams[1], local_grams[2], local_grams[3]), "wide")
    orthos, rights = ([], [])
    for full_grad, piece, gram in zip(fulls, left_mean, grams):
        cholesky_factor = jnp.linalg.cholesky(gram)
        orthonormal = jnp.swapaxes(
            jax.scipy.linalg.solve_triangular(
                cholesky_factor, jnp.swapaxes(piece, 1, 2), lower=True
            ),
            1,
            2,
        )
        orthos.append(orthonormal)
        rights.append(jnp.einsum("knm,knq->kmq", full_grad, orthonormal, precision=FULL_PRECISION))
    right_sums = lax.psum((rights[0], rights[1], rights[2], rights[3]), ("rep", "wide"))
    reduced, new_errors, new_factors = ([], [], [])
    for full_grad, orthonormal, right_sum in zip(fulls, orthos, right_sums):
        right_mean = right_sum / replicas
        approx = jnp.einsum("knq,kmq->knm", orthonormal, right_mean, precision=FULL_PRECISION)
        reduced.append(approx)
        new_errors.append((full_grad - approx)[None])
        new_factors.append(right_mean)
    reduced.append(summed[4] / replicas)
    masters = (attn_in, attn_out, ffn_in, ffn_out, small_params)
    momenta = (attn_in_mom, attn_out_mom, ffn_in_mom, ffn_out_mom, small_mom)
    averages = (attn_in_avg, attn_out_avg, ffn_in_avg, ffn_out_avg, small_avg)
    rates = (LEARN_RATE, LEARN_RATE, LEARN_RATE, LEARN_RATE, VECTOR_RATE)
    new_weights, new_momenta, new_averages = ([], [], [])
    for master, moment, average, update, rate in zip(masters, momenta, averages, reduced, rates):
        moment_new = MOMENTUM * moment + update
        weight_new = master - rate * moment_new
        new_weights.append(weight_new)
        new_momenta.append(moment_new)
        new_averages.append(average + AVERAGE * (weight_new - average))
    return (
        layer_out[None],
        input_grad[None],
        new_weights[0],
        new_weights[1],
        new_weights[2],
        new_weights[3],
        new_weights[4],
        new_momenta[0],
        new_momenta[1],
        new_momenta[2],
        new_momenta[3],
        new_momenta[4],
        new_errors[0],
        new_errors[1],
        new_errors[2],
        new_errors[3],
        new_factors[0],
        new_factors[1],
        new_factors[2],
        new_factors[3],
        new_averages[0],
        new_averages[1],
        new_averages[2],
        new_averages[3],
        new_averages[4],
    )


def solution(mesh):
    placed = (
        P(("rep", "wide"), None, None),
        P(("rep", "wide"), None, None),
        P(("rep", "wide"), None, None),
        P(("rep", "wide"), None),
        P(("rep", "wide"), None),
        P(("rep", "wide"), None),
        P(("rep", "wide"), None, None),
        P(None, "wide", None),
        P(None, "wide", None),
        P(None, "wide", None),
        P(None, "wide", None),
        P(None, "wide"),
        P(None, "wide", None),
        P(None, "wide", None),
        P(None, "wide", None),
        P(None, "wide", None),
        P(None, "wide"),
        P("rep", None, "wide", None),
        P("rep", None, "wide", None),
        P("rep", None, "wide", None),
        P("rep", None, "wide", None),
        P(),
        P(),
        P(),
        P(),
        P(None, "wide", None),
        P(None, "wide", None),
        P(None, "wide", None),
        P(None, "wide", None),
        P(None, "wide"),
    )
    return jax.shard_map(
        body,
        mesh=mesh,
        in_specs=placed,
        out_specs=(
            P(("rep", "wide"), None, None),
            P(("rep", "wide"), None, None),
            P(None, "wide", None),
            P(None, "wide", None),
            P(None, "wide", None),
            P(None, "wide", None),
            P(None, "wide"),
            P(None, "wide", None),
            P(None, "wide", None),
            P(None, "wide", None),
            P(None, "wide", None),
            P(None, "wide"),
            P("rep", None, "wide", None),
            P("rep", None, "wide", None),
            P("rep", None, "wide", None),
            P("rep", None, "wide", None),
            P(),
            P(),
            P(),
            P(),
            P(None, "wide", None),
            P(None, "wide", None),
            P(None, "wide", None),
            P(None, "wide", None),
            P(None, "wide"),
        ),
        check_vma=False,
    )
```

time: 862 us -> 770 us (0.89); the launches traced: 851 us -> 768 us
  matrix products: 472 us -> 32.4 us
  waiting for transfers between devices: 172 us -> 409 us
  Pallas kernels: 0 us -> 126 us
  blocking collectives: 100 us -> 138 us
  other arithmetic: 69.7 us -> 37.5 us
  local copies, waits for them, and re-layouts: 19.9 us -> 10.3 us
    dot_general x52 -> x0, matrix products: 441 us -> none  [the longest x4 127 us: attend_backward(): jnp.einsum('hqk,qhd->khd', score_grad, rows_query, preferred_element_type...]
    reduce_scatter x4 -> x6, waiting for transfers between devices: 45.5 us -> 198 us  [scatter(): lax.psum_scatter(rows, 'wide', scatter_dimension=0, tiled=True).astype(F32)]
    pallas_call x0 -> x1, Pallas kernels: none -> 126 us  [run_layer(): pl.pallas_call(layer_kernel, out_shape=(sds((length, width), BF), sds((le...]
    all_gather x4, waiting for transfers between devices: 10 us -> 67.9 us  [gather(): return lax.all_gather(rows.astype(BF), 'wide', axis=0, tiled=True)]
    all_gather x1 -> x3, blocking collectives: 14.4 us -> 49.3 us  [the longest x2 35 us: gather(): return lax.all_gather(rows.astype(BF), 'wide', axis=0, tiled=True)]
    unnamed x11 -> x13, waiting for transfers between devices: 0.16 us -> 24.7 us
    reduce_sum x11 -> x0, other arithmetic: 24.3 us -> none  [the longest x4 18.9 us: attend_forward(): row_total = jnp.sum(exponent, axis=-1, keepdims=True)]
    unnamed x153 -> x63, local copies, waits for them, and re-layouts: 16.8 us -> 3.23 us
  transfers between devices with their start and end apart: 10 -> 12, of which waited for: 4 -> 11; matrix products, arithmetic and copies ran while one was open for 48% -> 2% of each run, Pallas kernels for 0% -> 0%
where the time goes in v1:
time: 770 us; the launch traced here: 768 us
  waiting for transfers between devices  409 us (53%)
  blocking collectives  138 us (18%)
  Pallas kernels  126 us (16%)
  other arithmetic  37.5 us (5%)
  matrix products  32.4 us (4%)
  between operations  14.6 us (2%)
  local copies, waits for them, and re-layouts  10.3 us (1%)
    reduce_scatter x6, waiting for transfers between devices, scatter(): lax.psum_scatter(rows, 'wide', scatter_dimension=0, tiled=True).astype(F32)  198 us
    pallas_call x1, Pallas kernels, run_layer(): pl.pallas_call(layer_kernel, out_shape=(sds((length, width), BF), sds((le...  126 us
    psum x1, waiting for transfers between devices, body(): lax.psum((rights[0], rights[1], rights[2], rights[3]), ('rep', 'wide'))  118 us
    all_gather x4, waiting for transfers between devices, gather(): return lax.all_gather(rows.astype(BF), 'wide', axis=0, tiled=True)  67.9 us
    psum x1, blocking collectives, body(): lax.psum((rights[0], rights[1], rights[2], rights[3]), ('rep', 'wide'))  43.3 us
    all_gather x2, blocking collectives, gather(): return lax.all_gather(rows.astype(BF), 'wide', axis=0, tiled=True)  35 us
    psum x1, blocking collectives, body(): lax.psum((local_grams[0], local_grams[1], local_grams[2], local_grams[3])...  27.1 us
    unnamed x13, waiting for transfers between devices  24.7 us
  transfers between devices with their start and end apart: 12, of which 11 were waited for; matrix products, arithmetic and copies ran while one was open for 2% of the time, Pallas kernels for 0%

profile of v1, /device:TPU:8, one launch (start us, length us, event | category | flops | bytes accessed | tf_op | source)
XLA Modules:
  0.0 768.4 jit_solution(1053096366995760467)
XLA Ops:
  7.3 1.3 convert.16
  11.8 14.3 %all-gather.4 = bf16[8,64,11]{1,2,0:T(8,128)(2,1)S(1)} all-gather(bf16[1,64,11]{1,2,0:T(8,128)(2,1)S(1)} %convert_bitcast_fusion), channel_id=1, replica_groups=mesh['rep'=4,'wide'=8] {'wide'}, dimensions={0}, use_global_device_ids=true | all-gather | bytes 12672 | tf_op jit(solution)/shard_map/all_gather | solution.py:362
  26.9 17.1 %all-gather = bf16[1,512,512]{2,1,0:T(8,128)(2,1)} all-gather(bf16[1,64,512]{2,1,0:T(8,128)(2,1)S(1)} %get-tuple-element.77), channel_id=2, replica_groups=mesh['rep'=4,'wide'=8] {'wide'}, dimensions={1}, use_global_device_ids=true | all-gather | bytes 589824 | tf_op jit(solution)/shard_map/all_gather | solution.py:370
  44.0 17.9 %all-gather.1 = bf16[1,512,512]{2,1,0:T(8,128)(2,1)} all-gather(bf16[1,64,512]{2,1,0:T(8,128)(2,1)S(1)} %get-tuple-element.76), channel_id=3, replica_groups=mesh['rep'=4,'wide'=8] {'wide'}, dimensions={1}, use_global_device_ids=true | all-gather | bytes 589824 | tf_op jit(solution)/shard_map/all_gather | solution.py:370
  61.9 6.1 all-gather.12.cloned.1.call-done.wa2
  68.0 31.1 %all-gather.14.cloned.1.call-done = bf16[1,512,2048]{2,1,0:T(8,128)(2,1)} async-done(((bf16[1,64,2048]{2,1,0:T(8,128)(2,1)}), bf16[1,512,2048]{2,1,0:T(8,128)(2,1)}) %all-gather.14.cloned.1.call-update) | async-done | bytes 2097168 | tf_op jit(solution)/shard_map/all_gather | solution.py:370
  99.2 30.7 %all-gather.16.cloned.1.call-done = bf16[1,2048,512]{2,1,0:T(8,128)(2,1)} async-done(((bf16[1,256,512]{2,1,0:T(8,128)(2,1)}), bf16[1,2048,512]{2,1,0:T(8,128)(2,1)}) %all-gather.16.cloned.1.call-update) | async-done | bytes 2097168 | tf_op jit(solution)/shard_map/all_gather | solution.py:370
  129.8 126.2 %layer.1 = (bf16[1024,512]{1,0:T(8,128)(2,1)}, f32[1024,512]{1,0:T(8,128)}, bf16[512,2048]{1,0:T(8,128)(2,1)}, bf16[2048,512]{1,0:T(8,128)(2,1)}, bf16[512,512]{...) custom-call(s32[1,1024]{1,0:T(1,128)} %sid.1, ...), custom_call_target="tpu_custom_call" | custom-call | tf_op jit(solution)/shard_map/layer/pallas_call | solution.py:307
  256.0 1.6 copy.148
  263.3 20.8 %reduce-scatter.22.cloned.1.call-done = f32[64,11]{1,0:T(8,128)} async-done(((f32[512,11]{1,0:T(8,128)}), f32[64,11]{1,0:T(8,128)}) %reduce-scatter.22.cloned.1.call-update) | async-done | bytes 2832
  285.6 30.5 %reduce-scatter.14.cloned.1.call-done = bf16[64,512]{1,0:T(8,128)(2,1)} async-done(((bf16[512,512]{1,0:T(8,128)(2,1)}), bf16[64,512]{1,0:T(8,128)(2,1)}) %reduce-scatter.14.cloned.1.call-update) | async-done | bytes 65552 | tf_op jit(solution)/shard_map/reduce_scatter | solution.py:384
  316.0 31.9 %reduce-scatter.16.cloned.1.call-done = bf16[64,512]{1,0:T(8,128)(2,1)} async-done(((bf16[512,512]{1,0:T(8,128)(2,1)}), bf16[64,512]{1,0:T(8,128)(2,1)}) %reduce-scatter.16.cloned.1.call-update) | async-done | bytes 65552 | tf_op jit(solution)/shard_map/reduce_scatter | solution.py:384
  347.9 1.8 fusion.53
  349.8 32.8 %reduce-scatter.12.cloned.1.call-done = bf16[64,1536]{1,0:T(8,128)(2,1)} async-done(((bf16[512,1536]{1,0:T(8,128)(2,1)}), bf16[64,1536]{1,0:T(8,128)(2,1)}) %reduce-scatter.12.cloned.1.call-update) | async-done | bytes 196624 | tf_op jit(solution)/shard_map/reduce_scatter | solution.py:384
  382.6 0.9 copy.157
  383.6 33.8 %reduce-scatter.10.cloned.1.call-done = bf16[64,1536]{1,0:T(8,128)(2,1)} async-done(((bf16[512,1536]{1,0:T(8,128)(2,1)}), bf16[64,1536]{1,0:T(8,128)(2,1)}) %reduce-scatter.10.cloned.1.call-update) | async-done | bytes 196624 | tf_op jit(solution)/shard_map/reduce_scatter | solution.py:384
  417.3 0.9 copy.158
  419.1 34.3 %reduce-scatter.20.cloned.1.call-done = bf16[256,512]{1,0:T(8,128)(2,1)} async-done(((bf16[2048,512]{1,0:T(8,128)(2,1)}), bf16[256,512]{1,0:T(8,128)(2,1)}) %reduce-scatter.20.cloned.1.call-update) | async-done | bytes 262160 | tf_op jit(solution)/shard_map/reduce_scatter | solution.py:384
  453.5 2.2 convolution_bitcast_fusion.2
  455.6 34.9 %reduce-scatter.18.cloned.1.call-done = bf16[64,2048]{1,0:T(8,128)(2,1)} async-done(((bf16[512,2048]{1,0:T(8,128)(2,1)}), bf16[64,2048]{1,0:T(8,128)(2,1)}) %reduce-scatter.18.cloned.1.call-update) | async-done | bytes 262160 | tf_op jit(solution)/shard_map/reduce_scatter | solution.py:384
  490.5 2.2 convolution_bitcast_fusion.5
  492.7 18.0 %all-reduce.3 = (f32[6,64,8]{1,2,0:T(8,128)S(1)}, f32[1,64,8]{1,2,0:T(8,128)}, f32[2,64,8]{1,2,0:T(8,128)}, f32[1,256,8]{1,2,0:T(8,128)}, f32[11,64]{1,0:T(8,128)}) all-reduce(f32[6,64,8]{1,2,0:T(8,128)S(1)} %fusion.55, f32[1,64,8]{1,2,0:T(8,128)} %convolution_bitcast_fusion.5, ...), channel_id=1, replica_groups=mesh['rep'=4,'wide'=8] {'rep'}, use_global_device_ids=true, to_apply=%region_2.0 | all-reduce | flops 7360 | bytes 58880 | tf_op jit(solution)/shard_map/psum | solution.py:409
  510.9 1.5 fusion.23
  512.4 1.5 convolution_bitcast_fusion.3
  513.9 1.5 convolution_bitcast_fusion.4
  515.4 27.1 %all-reduce.2 = (f32[6,8,8]{1,2,0:T(8,128)}, f32[1,8,8]{1,2,0:T(8,128)}, f32[2,8,8]{1,2,0:T(8,128)}, f32[1,8,8]{1,2,0:T(8,128)}) all-reduce(f32[6,8,8]{1,2,0:T(8,128)S(1)} %fusion.7, f32[1,8,8]{1,2,0:T(8,128)} %convolution_bitcast_fusion.4, f32[2,8,8]{1,2,0:T(8,128)} %fusion.23, ...), channel_id=1, replica_groups=mesh['rep'=4,'wide'=8] {'wide'}, use_global_device_ids=true, to_apply=%region_3.0 | all-reduce | flops 640 | bytes 5120 | tf_op jit(solution)/shard_map/psum | solution.py:414
  544.0 1.3 fusion.29
  547.9 1.5 fusion.16
  550.9 1.4 custom-call.29
  553.9 1.3 custom-call.30
  557.0 1.7 convolution_bitcast_fusion.1
  558.8 43.3 %all-reduce = (f32[2,512,8]{1,2,0:T(8,128)}, f32[1,512,8]{1,2,0:T(8,128)}) all-reduce(f32[2,512,8]{1,2,0:T(8,128)S(1)} %fusion.52, f32[1,512,8]{1,2,0:T(8,128)} %convolution_bitcast_fusion.1), channel_id=1, replica_groups=mesh['rep'=4,'wide'=8] {'rep','wide'}, use_global_device_ids=true, to_apply=%region_13.0 | all-reduce | flops 12288 | bytes 98304 | tf_op jit(solution)/shard_map/psum | solution.py:427
  602.0 1.3 broadcast_multiply_fusion.3
  603.4 1.4 custom-call.34
  608.4 1.4 fusion.5
  609.8 5.0 custom-call.27
  615.7 1.4 select_bitcast_fusion
  617.0 5.2 custom-call.28
  622.2 1.0 fusion.3
  623.2 1.2 fusion.54
  624.4 1.4 broadcast_multiply_fusion.2
  625.8 1.1 convolution_bitcast_fusion
  626.9 3.3 multiply_add_fusion.2
  630.3 1.4 multiply_add_fusion.4
  633.3 118.2 %all-reduce.6.cloned.1.call-done = (f32[6,512,8]{1,2,0:T(8,128)}, f32[1,2048,8]{1,2,0:T(8,128)}) async-done(((f32[6,512,8]{1,2,0:T(8,128)}, f32[1,2048,8]{1,2,0:T(8,128)}), (f32[6,512,8]{1,2,0:T(8,128)}, f32[1,2048,8]{1,2,0:T(8,128)})) %all-reduce.6.cloned.1.call-update) | async-done | bytes 163856 | tf_op jit(solution)/shard_map/psum | solution.py:427
  752.3 0.9 broadcast_multiply_fusion
  753.2 3.3 multiply_add_fusion.3
  756.5 4.1 multiply_add_fusion
  (127 shorter events, 28.8 us)
Async XLA Ops:
  7.2 411.1 %copy-start = (f32[6,512,8]{1,2,0:T(8,128)S(1)}, f32[6,512,8]{1,2,0:T(8,128)}, u32[]{:S(2)}) copy-start(f32[6,512,8]{1,2,0:T(8,128)} %param.52) | copy-start | bytes 294916
  7.2 2.9 copy-start.10
  7.2 3.7 copy-start.9
  7.2 54.6 %all-gather.10.cloned.1.call-start = ((), (), s32[]{:S(2)}) async-start(), calls=%async_computation.7 | async-start | bytes 1769472 | tf_op jit(solution)/shard_map/all_gather | solution.py:370
  8.6 3.2 copy-start.11
  8.6 3.3 copy-start.23
  9.3 58.7 %all-gather.12.cloned.1.call-start = ((), (), s32[]{:S(2)}) async-start(), calls=%async_computation.8 | async-start | bytes 1769472 | tf_op jit(solution)/shard_map/all_gather | solution.py:370
  10.1 89.1 %all-gather.14.cloned.1.call-start = ((), (), s32[]{:S(2)}) async-start(), calls=%async_computation.15 | async-start | bytes 2359296 | tf_op jit(solution)/shard_map/all_gather | solution.py:370
  10.9 118.9 %all-gather.16.cloned.1.call-start = ((), (), s32[]{:S(2)}) async-start(), calls=%async_computation.16 | async-start | bytes 2359296 | tf_op jit(solution)/shard_map/all_gather | solution.py:370
  11.7 272.4 %reduce-scatter.22.cloned.1.call-start = ((), (), s32[]{:S(2)}) async-start(), calls=%async_computation.17 | async-start | bytes 294912
  257.7 58.4 %reduce-scatter.14.cloned.1.call-start = ((), (), s32[]{:S(2)}) async-start(), calls=%async_computation.11 | async-start | bytes 589824 | tf_op jit(solution)/shard_map/reduce_scatter | solution.py:384
  258.2 89.7 %reduce-scatter.16.cloned.1.call-start = ((), (), s32[]{:S(2)}) async-start(), calls=%async_computation.12 | async-start | bytes 589824 | tf_op jit(solution)/shard_map/reduce_scatter | solution.py:384
  259.0 123.6 %reduce-scatter.12.cloned.1.call-start = ((), (), s32[]{:S(2)}) async-start(), calls=%async_computation.10 | async-start | bytes 1769472 | tf_op jit(solution)/shard_map/reduce_scatter | solution.py:384
  259.7 157.6 %reduce-scatter.10.cloned.1.call-start = ((), (), s32[]{:S(2)}) async-start(), calls=%async_computation.9 | async-start | bytes 1769472 | tf_op jit(solution)/shard_map/reduce_scatter | solution.py:384
  260.5 193.0 %reduce-scatter.20.cloned.1.call-start = ((), (), s32[]{:S(2)}) async-start(), calls=%async_computation.14 | async-start | bytes 2359296 | tf_op jit(solution)/shard_map/reduce_scatter | solution.py:384
  260.5 87.4 %copy-start.6 = (f32[1,2,64,512]{3,2,1,0:T(8,128)S(1)}, f32[1,2,64,512]{3,2,1,0:T(8,128)}, u32[]{:S(2)}) copy-start(f32[1,2,64,512]{3,2,1,0:T(8,128)} %param.49) | copy-start | bytes 786436
  260.5 87.4 %copy-start.25 = (f32[2,512,8]{1,2,0:T(8,128)S(1)}, f32[2,512,8]{1,2,0:T(8,128)}, u32[]{:S(2)}) copy-start(f32[2,512,8]{1,2,0:T(8,128)} %param.53) | copy-start | bytes 98308
  261.1 157.2 %copy-start.1 = (f32[1,6,64,512]{3,2,1,0:T(8,128)S(1)}, f32[1,6,64,512]{3,2,1,0:T(8,128)}, u32[]{:S(2)}) copy-start(f32[1,6,64,512]{3,2,1,0:T(8,128)} %param.48) | copy-start | bytes 2359300
  261.1 229.4 %reduce-scatter.18.cloned.1.call-start = ((), (), s32[]{:S(2)}) async-start(), calls=%async_computation.13 | async-start | bytes 2359296 | tf_op jit(solution)/shard_map/reduce_scatter | solution.py:384
  261.1 192.4 %copy-start.2 = (f32[1,1,256,512]{3,2,1,0:T(8,128)S(1)}, f32[1,1,256,512]{3,2,1,0:T(8,128)}, u32[]{:S(2)}) copy-start(f32[1,1,256,512]{3,2,1,0:T(8,128)} %param.51) | copy-start | bytes 1572868
  261.1 192.3 %copy-start.26 = (f32[1,512,8]{1,2,0:T(8,128)S(1)}, f32[1,512,8]{1,2,0:T(8,128)}, u32[]{:S(2)}) copy-start(f32[1,512,8]{1,2,0:T(8,128)} %param.55) | copy-start | bytes 49156
  261.8 228.7 %copy-start.3 = (f32[1,1,64,2048]{3,2,1,0:T(8,128)S(1)}, f32[1,1,64,2048]{3,2,1,0:T(8,128)}, u32[]{:S(2)}) copy-start(f32[1,1,64,2048]{3,2,1,0:T(8,128)} %param.50) | copy-start | bytes 1572868
  261.8 489.6 %all-reduce.6.cloned.1.call-start = ((), (), s32[]{:S(2)}) async-start(), calls=%async_computation.18 | async-start | bytes 327680 | tf_op jit(solution)/shard_map/psum | solution.py:427
  349.8 206.9 %copy-start.12 = (bf16[64,512]{1,0:T(8,128)(2,1)S(1)}, bf16[64,512]{1,0:T(8,128)(2,1)}, u32[]{:S(2)}) copy-start(bf16[64,512]{1,0:T(8,128)(2,1)} %reduce-scatter.14.cloned.1.call-done) | copy-start | bytes 196612
  349.8 206.9 %copy-start.13 = (bf16[64,512]{1,0:T(8,128)(2,1)S(1)}, bf16[64,512]{1,0:T(8,128)(2,1)}, u32[]{:S(2)}) copy-start(bf16[64,512]{1,0:T(8,128)(2,1)} %reduce-scatter.16.cloned.1.call-done) | copy-start | bytes 196612
  453.5 103.5 %copy-start.5 = (bf16[256,512]{1,0:T(8,128)(2,1)S(1)}, bf16[256,512]{1,0:T(8,128)(2,1)}, u32[]{:S(2)}) copy-start(bf16[256,512]{1,0:T(8,128)(2,1)} %reduce-scatter.20.cloned.1.call-done) | copy-start | bytes 786436
  490.5 135.3 %copy-start.7 = (bf16[64,2048]{1,0:T(8,128)(2,1)S(1)}, bf16[64,2048]{1,0:T(8,128)(2,1)}, u32[]{:S(2)}) copy-start(bf16[64,2048]{1,0:T(8,128)(2,1)} %reduce-scatter.18.cloned.1.call-done) | copy-start | bytes 786436
  510.7 44.5 %copy-start.19 = (f32[6,64,8]{1,2,0:T(8,128)}, f32[6,64,8]{1,2,0:T(8,128)S(1)}, u32[]{:S(2)}) copy-start(f32[6,64,8]{1,2,0:T(8,128)S(1)} %get-tuple-element.52) | copy-start | bytes 36868
  556.1 0.6 copy-start.21
  556.7 70.2 %copy-start.20 = (f32[8,256]{1,0:T(8,128)S(1)}, f32[8,256]{1,0:T(8,128)}, u32[]{:S(2)}) copy-start(f32[8,256]{1,0:T(8,128)} %fusion.16) | copy-start | bytes 24580
  626.9 3.4 copy-start.16
  626.9 3.4 copy-start.22
  626.9 3.3 copy-start.17
  626.9 3.3 copy-start.18
  630.3 2.4 copy-start.24
  630.3 2.4 copy-start.27
  630.3 2.4 copy-start.28
  630.3 2.4 copy-start.29
  632.7 123.8 %copy-start.4 = (f32[6,64,512]{2,1,0:T(8,128)S(1)}, f32[6,64,512]{2,1,0:T(8,128)}, u32[]{:S(2)}) copy-start(f32[6,64,512]{2,1,0:T(8,128)} %param.38) | copy-start | bytes 2359300
  752.3 8.3 %copy-start.15 = (f32[1,2048,8]{1,2,0:T(8,128)}, f32[1,2048,8]{1,2,0:T(8,128)S(1)}, u32[]{:S(2)}) copy-start(f32[1,2048,8]{1,2,0:T(8,128)S(1)} %broadcast_multiply_fusion.1) | copy-start | bytes 196612
  753.2 7.4 copy-start.14
  756.5 4.1 copy-start.8
Sparse Core Ops, SparseCore 0:
  10.3 27.8 all-gather.9
  40.4 27.6 all-gather.11
  70.2 28.9 all-gather.13
  101.2 28.5 all-gather.15
  257.8 26.2 reduce-scatter.21
  286.9 29.0 reduce-scatter.13
  318.9 29.0 reduce-scatter.15
  350.3 32.2 reduce-scatter.11
  385.0 32.2 reduce-scatter.9
  419.6 33.8 reduce-scatter.19
  455.9 34.5 reduce-scatter.17
  627.0 124.3 all-reduce.5
